TPU v7x, 512 devices: a whole 4x4x16 slice. The times are simulated.
512 devices in a mesh: blk: 32 (over z_lo, x), pen: 16 (over z_hi, y, core).
Axes of the slice: x: 4, y: 4, z: 16 (z_hi: 2, z_lo: 8; z = z_hi * 8 + z_lo), core: 2. Of those that a mesh axis runs over, the one named last changes fastest.
Arguments:
- state: float32 [32, 128, 5, 1024], P('blk', 'pen'), may hold values from -6 to 6
- previous: float32 [32, 128, 5, 1024], P('blk', 'pen'), may hold values from -6 to 6
- iblank: int32 [32, 128, 1024], P('blk', 'pen'), may hold values 0 or 1
- block_owner: int32 [32], replicated, may hold values from 0 to 31, as said below
- donor_cell: int32 [16, 32, 32, 128, 8], P('pen', 'blk'), may hold values from 0 to 8191
- donor_weight: float32 [16, 32, 32, 128, 8], P('pen', 'blk'), may hold values from 0.02 to 0.25
- send_count: int32 [16, 32, 32], P('pen', 'blk'), may hold values from 0 to 128, as said below
- recv_cell: int32 [16, 32, 32, 128], P('pen', 'blk'), may hold values from 0 to 8191, as said below
- speed: float32 [32, 5, 1024], P('blk'), may hold values from -1 to 1
- left_vectors: float32 [32, 5, 5, 1024], P('blk'), may hold values from -2.5 to 2.5
- right_vectors: float32 [32, 5, 5, 1024], P('blk'), may hold values from -2.5 to 2.5
- line_inverse: float32 [32, 5, 128, 128], P('blk')
Outputs:
- updated: float32 [32, 128, 5, 1024], P('blk', 'pen')
Inputs may be any that keep to these rules, and one draw needn't show every extreme that they name: `block_owner`: each device holds exactly one block. `donor_cell`: donor cells lie among the slab's first min(8192, 16368) cells. Slots at or past the live count hold valid cell numbers that are not used. `send_count`: A device sends no rows to its own block. At most 128 rows go from one device to one block; in every draw each device sends exactly 128 rows to some block of each slab. `recv_cell`: for one device and slab, the cells of all slots over all sending blocks are distinct.
All inputs are finite; a program needn't handle non-finite values. No bound on the sum of `iblank` on one device may be relied on, other than what follows from the above.
Results may differ from a plain program's by a relative error of at most 0.0001.
Values sent between devices are 32-bit elements; how exact they have to be, the bound alone decides.
A program may use at most 192 MiB of HBM per device.

v0:
```python
import jax
import jax.numpy as jnp
from jax import lax
from jax.sharding import PartitionSpec as P


def padded_2(cells, sides, width):
    for axis, dim in sides:
        count = lax.axis_size(axis)
        ends = count - 1
        head = lax.slice_in_dim(cells, 0, width, axis=dim)
        tail = lax.slice_in_dim(cells, cells.shape[dim] - width, cells.shape[dim], axis=dim)
        cells = jnp.concatenate(
            [
                lax.ppermute(tail, axis, [(i, (i + 1) % count) for i in range(ends)]),
                cells,
                lax.ppermute(head, axis, [((i + 1) % count, i) for i in range(ends)]),
            ],
            axis=dim,
        )
    return cells


def shards(
    state,
    previous,
    iblank,
    block_owner,
    donor_cell,
    donor_weight,
    send_count,
    recv_cell,
    speed,
    left_vectors,
    right_vectors,
    line_inverse,
):
    current = state[0]
    depth, nfields, pencils = current.shape
    ncells = depth * pencils
    nblocks = block_owner.shape[0]
    high = lax.Precision.HIGHEST
    flat = current.transpose(1, 0, 2).reshape(nfields, ncells)
    blocks = jnp.arange(nblocks, dtype=jnp.int32)
    match = block_owner[:, None] == blocks[None, :]
    held = jnp.sum(jnp.where(match, blocks[:, None], 0), axis=0)
    cells = donor_cell[0, 0]
    weights = donor_weight[0, 0]
    picked = flat[:, cells]
    counts_out = send_count[0, 0][held].astype(jnp.float32)
    rows_out = jnp.sum(picked * weights[None], axis=-1).transpose(1, 0, 2)[held]
    arrived, counts_in = (
        lax.all_to_all(rows_out, "blk", split_axis=0, concat_axis=0, tiled=True),
        lax.all_to_all(counts_out, "blk", split_axis=0, concat_axis=0, tiled=True),
    )
    by_block = arrived[block_owner]
    live_counts = counts_in[block_owner].astype(jnp.int32)
    slots = jnp.arange(by_block.shape[-1], dtype=jnp.int32)
    live = slots[None, :] < live_counts[:, None]
    target = jnp.where(live, recv_cell[0, 0], ncells)
    incoming = by_block.transpose(1, 0, 2).reshape(nfields, -1)
    flat = flat.at[:, target.reshape(-1)].set(incoming, mode="drop")
    filled = flat.reshape(nfields, depth, pencils).transpose(1, 0, 2)
    padded = padded_2(filled, (("pen", 0),), 2)
    upper = padded[3:-1]
    lower = padded[1:-3]
    upper_two = padded[4:]
    lower_two = padded[:-4]
    wave = speed[0][None]
    resid = -(filled - previous[0]) - 0.5 * wave * (upper - lower)
    resid = resid + 0.25 * (upper - 2.0 * filled + lower)
    resid = resid - 0.0625 * (upper_two - 4.0 * upper + 6.0 * filled - 4.0 * lower + lower_two)
    resid = resid - 0.25 * (jnp.roll(filled, -1, axis=-1) - jnp.roll(filled, 1, axis=-1))
    keep = iblank[0].astype(jnp.float32)[:, None, :]
    resid = resid * keep
    work = jnp.einsum("mnp,jnp->jmp", left_vectors[0], resid, precision=high)
    inverse = line_inverse[0]
    position = lax.axis_index("pen") * depth
    own_rows = lax.dynamic_slice_in_dim(inverse, position, depth, 1)
    solved = jnp.einsum(
        "mjk,kmp->jmp", own_rows, lax.all_gather(work, "pen", axis=0, tiled=True), precision=high
    )
    change = jnp.einsum("mnp,jnp->jmp", right_vectors[0], solved, precision=high)
    return (filled + keep * change)[None]


def solution(mesh):
    placed = (
        P("blk", "pen", None, None),
        P("blk", "pen", None, None),
        P("blk", "pen", None),
        P(),
        P("pen", "blk", None, None, None),
        P("pen", "blk", None, None, None),
        P("pen", "blk", None),
        P("pen", "blk", None, None),
        P("blk", None, None),
        P("blk", None, None, None),
        P("blk", None, None, None),
        P("blk", None, None, None),
    )
    return jax.shard_map(
        shards, mesh=mesh, in_specs=placed, out_specs=P("blk", "pen", None, None), check_vma=False
    )
```

profile of v0, /device:TPU:97, one launch (start us, length us, event | category | flops | bytes accessed | tf_op | source)
XLA Modules:
  0.0 1383.7 jit_solution(2545792803028667019)
XLA Ops:
  6.5 0.8 select_reduce_fusion
  7.4 1.4 gather_fusion
  8.7 0.7 copy.165
  9.4 13.8 all-to-all-start
  23.2 0.7 compare_select_fusion.2
  23.9 3.6 copy.164
  28.1 1.0 reshape.134
  29.8 111.2 %gather_fusion.2 = f32[32768,5]{1,0:T(8,128)} fusion(f32[5,8192]{0,1:T(8,128)} %bitcast.80, s32[32768]{0:T(1024)S(1)} %broadcast_clamp_fusion), kind=kCustom, calls=%fused_computation.2 | custom fusion | bytes 1441792 | tf_op jit(solution)/shard_map/gather | solution.py:49
  141.0 11.8 multiply_reduce_fusion
  152.8 2.2 copy.168
  155.0 1.3 gather_fusion.3
  156.3 2.7 copy.178
  159.0 12.0 all-to-all-start.1
  171.4 0.7 gather_fusion.1
  172.2 8.1 all-to-all-done.1
  180.9 0.6 copy.169
  181.6 14.7 %scatter_fusion = f32[5,8192]{0,1:T(8,128)} fusion(f32[5,8192]{0,1:T(8,128)} %bitcast.81, s32[4096]{0:T(1024)S(1)} %bitcast.93, f32[4096,5]{1,0:T(8,128)S(1)} %copy.169), kind=kCustom, calls=%fused_computation.5 | custom fusion | bytes 262144 | tf_op jit(solution)/shard_map/scatter | solution.py:62
  196.3 2.9 copy.177
  199.3 5.2 collective-permute-start
  204.5 3.3 collective-permute-start.1
  207.9 0.8 collective-permute-done.1
  209.0 2.8 copy.171
  211.7 12.4 fusion.4
  224.1 0.9 copy-done.5
  225.0 2.7 copy.179
  227.7 1090.4 %all-gather.2.cloned.1.call-done = f32[128,5,1024]{1,0,2:T(8,128)} async-done(((f32[8,5,1024]{1,0,2:T(8,128)}), f32[128,5,1024]{1,0,2:T(8,128)}) %all-gather.2.cloned.1.call-update) | async-done | bytes 2621456 | tf_op jit(solution)/shard_map/all_gather | solution.py:81
  1318.1 38.6 %copy.173 = f32[128,5,1024]{2,0,1:T(8,128)S(1)} copy(f32[128,5,1024]{1,0,2:T(8,128)} %all-gather.2.cloned.1.call-done) | data formatting | bytes 5242880 | tf_op jit(solution)/shard_map/all_gather | solution.py:81
  1356.7 1.5 convolution_bitcast_fusion
  1358.2 2.8 copy.174
  1360.9 12.3 fusion
  1373.3 2.9 copy.176
  1376.2 0.7 fusion.19
  (41 shorter events, 2.9 us)
Async XLA Ops:
  6.5 1350.1 %copy-start = (f32[1,5,128,128]{3,2,1,0:T(8,128)S(1)}, f32[1,5,128,128]{3,2,1,0:T(8,128)}, u32[]{:S(2)}) copy-start(f32[1,5,128,128]{3,2,1,0:T(8,128)} %param.23) | copy-start | bytes 983044
  6.5 20.9 %copy-start.3 = (s32[1,1,32,128,8]{3,4,2,1,0:T(8,128)S(1)}, s32[1,1,32,128,8]{3,4,2,1,0:T(8,128)}, u32[]{:S(2)}) copy-start(s32[1,1,32,128,8]{3,4,2,1,0:T(8,128)} %param.16) | copy-start | bytes 393220
  9.4 149.6 %all-to-all-start = ((f32[32,1,1]{2,1,0:T(1,128)}), f32[32,1,1]{2,1,0:T(1,128)S(1)}, u32[]{:S(2)}, u32[]{:S(2)}) async-start(f32[32,1,1]{2,1,0:T(1,128)} %copy.165), calls=%async_computation | async-start | bytes 32768 | tf_op jit(solution)/shard_map/all_to_all | solution.py:54
  23.9 5.3 copy-start.2
  27.4 2.3 copy-start.6
  27.4 2.3 copy-start.7
  141.0 15.3 %copy-start.4 = (f32[1,5,5,1024]{3,0,2,1:T(1,128)S(1)}, f32[1,5,5,1024]{3,0,2,1:T(1,128)}, u32[]{:S(2)}) copy-start(f32[1,5,5,1024]{3,0,2,1:T(1,128)} %param.21) | copy-start | bytes 307204
  152.8 19.3 %copy-start.8 = (s32[1,1,32,128]{3,2,1,0:T(8,128)S(1)}, s32[1,1,32,128]{3,2,1,0:T(8,128)}, u32[]{:S(2)}) copy-start(s32[1,1,32,128]{3,2,1,0:T(8,128)} %param.19) | copy-start | bytes 49156
  159.0 21.3 %all-to-all-start.1 = ((f32[32,5,128]{2,1,0:T(8,128)}), f32[32,5,128]{2,1,0:T(8,128)S(1)}, u32[]{:S(2)}, u32[]{:S(2)}) async-start(f32[32,5,128]{2,1,0:T(8,128)} %gather_fusion.3), calls=%async_computation.1 | async-start | bytes 262144 | tf_op jit(solution)/shard_map/all_to_all | solution.py:53
  171.0 1147.1 %all-gather.2.cloned.1.call-start = ((), (), s32[]{:S(2)}) async-start(), calls=%async_computation.2 | async-start | bytes 71303168 | tf_op jit(solution)/shard_map/all_gather | solution.py:81
  181.6 27.2 %copy-start.1 = (f32[1,8,5,1024]{3,1,2,0:T(8,128)S(1)}, f32[1,8,5,1024]{3,1,2,0:T(8,128)}, u32[]{:S(2)}) copy-start(f32[1,8,5,1024]{3,1,2,0:T(8,128)} %param.13) | copy-start | bytes 491524
  199.3 8.6 collective-permute-start
  204.5 4.2 collective-permute-start.1
  224.1 0.9 copy-start.5
Sparse Core Ops, SparseCore 0:
  224.2 1093.7 all-gather.1
where the time goes:
time: 1380 us
  waiting for transfers between devices  1100 us (80%)
  local copies, waits for them, and re-layouts  195 us (14%)
  starting transfers between devices  34.3 us (2%)
  matrix products  26.2 us (2%)
  other arithmetic  14.7 us (1%)
    all_gather x1, waiting for transfers between devices, shards(): lax.all_gather(work, 'pen', axis=0, tiled=True)  1090 us
    gather x1, local copies, waits for them, and re-layouts, shards(): picked = flat[:, cells]  111 us
    all_gather x1, local copies, waits for them, and re-layouts, shards(): lax.all_gather(work, 'pen', axis=0, tiled=True)  38.6 us
  transfers between devices with their start and end apart: 5, of which 3 were waited for; matrix products, arithmetic and copies ran while one was open for 10% of the time, Pallas kernels for 0%

commit v1 on v0

v1 whole, which is shorter than its diff:
```python
import functools

import jax
import jax.numpy as jnp
from jax import lax
from jax.experimental import pallas as pl
from jax.experimental.pallas import tpu as pltpu
from jax.sharding import PartitionSpec as P

MESH = pl.DeviceIdType.MESH
LANES = 128
DEAD = 1e30
TOGETHER = 4
INVERTED = 4


def lane_pick(table, index):
    return jnp.take_along_axis(table, index, axis=1, mode="promise_in_bounds")


def log2(n):
    assert n & (n - 1) == 0
    return n.bit_length() - 1


def kernel(
    n_blk,
    n_pen,
    owner_hbm,
    count_hbm,
    state_hbm,
    prev_hbm,
    iblank_hbm,
    dcell_hbm,
    dweight_hbm,
    rcell_hbm,
    speed_hbm,
    left_hbm,
    right_hbm,
    linv_hbm,
    out_ref,
    owner_ref,
    count_ref,
    state_ref,
    prev_ref,
    iblank_ref,
    dcell_ref,
    dweight_ref,
    rcell_ref,
    speed_ref,
    left_ref,
    right_ref,
    linv_ref,
    load_sem,
    held_vec,
    held_ref,
    held_sem,
    inv_ref,
    rows_out,
    rows_in,
    filled,
    halo_out,
    halo_in,
    resid,
    work,
    parts_in,
    work_line,
    solved_line,
    solved,
    fringe_send,
    fringe_recv,
    halo_send,
    halo_recv,
    fwd_send,
    fwd_recv,
    back_send,
    back_recv,
):
    nf, depth, pencils = state_hbm.shape
    groups = pencils // LANES
    n_a = n_pen // 2
    assert n_a == groups and depth == 8 and nf == 5
    n_hi = groups * depth
    p_bits, g_bits = log2(pencils), log2(groups)
    f32, i32 = jnp.float32, jnp.int32

    me_b = lax.axis_index("blk")
    me_p = lax.axis_index("pen")
    zh = lax.div(me_p, n_a)
    a = lax.rem(me_p, n_a)
    third = lax.rem(a, 2) == zh

    def lane_group(g):
        return pl.ds(pl.multiple_of(g * LANES, LANES), LANES)

    @pl.when(me_p == 0)
    def _():
        halo_in[0] = jnp.zeros(halo_in.shape[1:], f32)

    @pl.when(me_p == n_pen - 1)
    def _():
        halo_in[1] = jnp.zeros(halo_in.shape[1:], f32)

    barrier = pltpu.get_barrier_semaphore()

    def greet_blk(off, _):
        pl.semaphore_signal(barrier, inc=1, device_id={"blk": lax.rem(me_b + off, n_blk)}, device_id_type=MESH)
        return 0

    def greet_pen(off, _):
        pl.semaphore_signal(barrier, inc=1, device_id={"pen": lax.rem(me_p + off, n_pen)}, device_id_type=MESH)
        return 0

    lax.fori_loop(1, n_blk, greet_blk, 0)
    lax.fori_loop(1, n_pen, greet_pen, 0)

    loads = {}
    for name, source, target in (
        ("rcell", rcell_hbm, rcell_ref),
        ("owner", owner_hbm, owner_ref),
        ("count", count_hbm, count_ref),
        ("state", state_hbm, state_ref),
        ("dcell", dcell_hbm, dcell_ref),
        ("dweight", dweight_hbm, dweight_ref),
        ("prev", prev_hbm, prev_ref),
        ("iblank", iblank_hbm, iblank_ref),
        ("speed", speed_hbm, speed_ref),
        ("left", left_hbm, left_ref),
        ("linv", linv_hbm, linv_ref),
        ("right", right_hbm, right_ref),
    ):
        loads[name] = pltpu.make_async_copy(source, target, load_sem.at[len(loads)])
        loads[name].start()

    def loaded(*names):
        for name in names:
            loads[name].wait()

    lane = lax.broadcasted_iota(i32, (1, LANES), 1)
    hi_iota = lax.broadcasted_iota(i32, (n_hi, LANES), 0)
    lo_iota = lax.broadcasted_iota(i32, (LANES, LANES), 0)

    def invert(step, acc):
        tall, flat = [], []
        for u in range(INVERTED):
            b = step * INVERTED + u
            c = rcell_ref[pl.ds(b, 1), :]
            j = lax.shift_right_logical(c, p_bits)
            g = lax.shift_right_logical(c, 7) & (groups - 1)
            at_hi = hi_iota == g * depth + j
            slot = jnp.where(at_hi, (lane + 1).astype(f32), 0.0)
            block = jnp.where(at_hi, (b + 1).astype(f32), 0.0)
            tall.append(jnp.concatenate([slot, block], axis=0).astype(jnp.bfloat16))
            flat.append(jnp.where(lo_iota == (c & (LANES - 1)), 1.0, 0.0).astype(jnp.bfloat16))
        return acc + lax.dot_general(
            jnp.concatenate(tall, axis=1),
            jnp.concatenate(flat, axis=1),
            (((1,), (1,)), ((), ())),
            preferred_element_type=f32,
        )

    loaded("owner")
    held = jnp.zeros((1, LANES), i32)
    for b in range(n_blk):
        held = jnp.where(lane == owner_ref[b], b, held)
    held_vec[...] = held
    held_copy = pltpu.make_async_copy(held_vec, held_ref, held_sem)
    held_copy.start()

    loaded("rcell")
    inv = lax.fori_loop(0, n_blk // INVERTED, invert, jnp.zeros((2 * n_hi, LANES), f32))
    inv = inv.astype(i32) - 1
    inv_ref[0] = jnp.maximum(inv[:n_hi], 0)
    inv_ref[1] = inv[n_hi:]
    held_copy.wait()

    loaded("count", "state", "dcell", "dweight")
    filled[...] = state_ref[...]

    pl.semaphore_wait(barrier, n_blk - 1 + n_pen - 1)

    def fringe_offset(i):
        return n_blk // 2 + lax.div(i + 1, 2) * (2 * lax.rem(i, 2) - 1)

    def fringe_copy(slot, peer, source):
        return pltpu.make_async_remote_copy(
            src_ref=rows_out.at[slot],
            dst_ref=rows_in.at[source],
            send_sem=fringe_send.at[slot],
            recv_sem=fringe_recv.at[source],
            device_id={"blk": peer},
            device_id_type=MESH,
        )

    def interpolate(q, _):
        peers, blocks, his, los = [], [], [], []
        for u in range(TOGETHER):
            peer = lax.rem(me_b + fringe_offset(q * TOGETHER + u), n_blk)
            block = held_ref[0, peer]
            cells = dcell_ref[block]
            peers.append(peer)
            blocks.append(block)
            his.append(lax.shift_right_logical(cells, 7))
            los.append(cells & (LANES - 1))

        def pick(g, acc):
            acc = [list(one) for one in acc]
            for j in range(depth):
                here = [hi == j * groups + g for hi in his]
                for m in range(nf):
                    table = jnp.broadcast_to(state_ref[m, j : j + 1, lane_group(g)], (8, LANES))
                    for u in range(TOGETHER):
                        acc[u][m] = jnp.where(here[u], lane_pick(table, los[u]), acc[u][m])
            return tuple(tuple(one) for one in acc)

        zero = jnp.zeros((8, LANES), f32)
        acc = lax.fori_loop(0, groups, pick, tuple(tuple(zero for _ in range(nf)) for _ in range(TOGETHER)))
        for u in range(TOGETHER):
            slot = q * TOGETHER + u
            weight = dweight_ref[blocks[u]]
            live = lane < count_ref[blocks[u]]
            for m in range(nf):
                row = jnp.sum(acc[u][m] * weight, axis=0, keepdims=True)
                if m == 0:
                    row = jnp.where(live, row, DEAD)
                rows_out[slot, pl.ds(m, 1), :] = row

            @pl.when(slot < n_blk - 1)
            def _():
                fringe_copy(slot, peers[u], me_b).start()

        return 0

    lax.fori_loop(0, n_blk // TOGETHER, interpolate, 0)

    def place(i, _):
        source = lax.rem(me_b - fringe_offset(i) + n_blk, n_blk)
        fringe_copy(i, source, source).wait_recv()
        block = held_ref[0, source]
        tables = [jnp.broadcast_to(rows_in[source, m : m + 1, :], (depth, LANES)) for m in range(nf)]
        for g in range(groups):
            lanes = slice(g * LANES, (g + 1) * LANES)
            slot = inv_ref[0, g * depth : (g + 1) * depth, :]
            first = lane_pick(tables[0], slot)
            here = (inv_ref[1, g * depth : (g + 1) * depth, :] == block) & (first < 0.5 * DEAD)
            for m in range(nf):
                value = first if m == 0 else lane_pick(tables[m], slot)
                filled[m, :, lanes] = jnp.where(here, value, filled[m, :, lanes])
        return 0

    lax.fori_loop(0, n_blk - 1, place, 0)

    def halo_copy(way, peer):
        return pltpu.make_async_remote_copy(
            src_ref=halo_out.at[way],
            dst_ref=halo_in.at[way],
            send_sem=halo_send.at[way],
            recv_sem=halo_recv.at[way],
            device_id={"pen": peer},
            device_id_type=MESH,
        )

    halo_out[0] = filled[:, depth - 2 :, :]
    halo_out[1] = filled[:, :2, :]
    upward = halo_copy(0, lax.rem(me_p + 1, n_pen))
    downward = halo_copy(1, lax.rem(me_p + n_pen - 1, n_pen))

    @pl.when(me_p < n_pen - 1)
    def _():
        upward.start()

    @pl.when(me_p > 0)
    def _():
        downward.start()

    loaded("prev", "iblank", "speed", "left")
    layer = lax.broadcasted_iota(i32, (depth, pencils), 0)
    keep = iblank_ref[...].astype(f32)

    def wave(m):
        return jnp.concatenate([speed_ref[m * groups + g : m * groups + g + 1, :] for g in range(groups)], axis=1)

    for m in range(nf):
        cur = filled[m]
        upper = jnp.where(layer == depth - 1, 0.0, pltpu.roll(cur, depth - 1, 0))
        upper_two = jnp.where(layer >= depth - 2, 0.0, pltpu.roll(cur, depth - 2, 0))
        lower = jnp.where(layer == 0, 0.0, pltpu.roll(cur, 1, 0))
        lower_two = jnp.where(layer <= 1, 0.0, pltpu.roll(cur, 2, 0))
        r = -(cur - prev_ref[m]) - 0.5 * wave(m) * (upper - lower)
        r = r + 0.25 * (upper - 2.0 * cur + lower)
        r = r - 0.0625 * (upper_two - 4.0 * upper + 6.0 * cur - 4.0 * lower + lower_two)
        r = r - 0.25 * (pltpu.roll(cur, pencils - 1, 1) - pltpu.roll(cur, 1, 1))
        resid[m] = r * keep

    def mix(matrix_ref, values_ref, m, g):
        lanes = slice(g * LANES, (g + 1) * LANES)
        total = None
        for n in range(nf):
            at = (m * nf + n) * groups + g
            term = matrix_ref[at : at + 1, :] * values_ref[n, :, lanes]
            total = term if total is None else total + term
        return total

    def slab_rows(p):
        return pl.ds(pl.multiple_of(p * depth, depth), depth)

    def each_peer(do):
        lax.fori_loop(0, n_a, lambda i, _: do(1 - zh, lax.rem(a + i, n_a)), 0)
        lax.fori_loop(1, n_a, lambda i, _: do(zh, lax.rem(a + i, n_a)), 0)

    def each_source(do):
        lax.fori_loop(1, n_a, lambda i, _: do(zh, lax.rem(a + n_a - i, n_a)), 0)
        lax.fori_loop(0, n_a, lambda i, _: do(1 - zh, lax.rem(a + n_a - i, n_a)), 0)

    def takes_third(half, g):
        return lax.rem(g, 2) == half

    def fwd_copy(message, half, g, source):
        first, lanes, peer = half * 2, lane_group(g), half * n_a + g
        src, dst = (
            lambda: (work.at[0, pl.ds(first, 2), :, lanes], parts_in.at[0, pl.ds(0, 2), source]),
            lambda: (work.at[1, first, :, lanes], parts_in.at[1, 0, source]),
            lambda: (work.at[1, first + 1, :, lanes], parts_in.at[1, 1, source]),
            lambda: (work.at[0, 4, :, lanes], parts_in.at[0, 2, source]),
            lambda: (work.at[1, 4, :, lanes], parts_in.at[1, 2, source]),
        )[message]()
        return pltpu.make_async_remote_copy(
            src_ref=src,
            dst_ref=dst,
            send_sem=fwd_send.at[message, peer],
            recv_sem=fwd_recv.at[message, source],
            device_id={"pen": peer},
            device_id_type=MESH,
        )

    def send_message(message):
        def send(half, g):
            if message < 3:
                fwd_copy(message, half, g, me_p).start()
            else:

                @pl.when(takes_third(half, g))
                def _():
                    fwd_copy(message, half, g, me_p).start()

            return 0

        each_peer(send)

    def keep_part(part):
        for f in range(3):
            field = 4 if f == 2 else zh * 2 + f
            parts_in[part, f, me_p] = work[part, field, :, lane_group(a)]

    for g in range(groups):
        for m in range(nf):
            work[0, m, :, g * LANES : (g + 1) * LANES] = mix(left_ref, resid, m, g)[2 : depth - 2, :]
    send_message(0)
    send_message(3)
    keep_part(0)

    @pl.when(me_p > 0)
    def _():
        upward.wait_recv()

    @pl.when(me_p < n_pen - 1)
    def _():
        downward.wait_recv()

    for m in range(nf):
        low2, low1 = halo_in[0, m, 0:1, :], halo_in[0, m, 1:2, :]
        up1, up2 = halo_in[1, m, 0:1, :], halo_in[1, m, 1:2, :]
        speed = wave(m)
        first = (0.5 + 0.5 * speed) * low1 - 0.0625 * low2
        last = (0.5 - 0.5 * speed) * up1 - 0.0625 * up2
        second, last_but = -0.0625 * low1, -0.0625 * up1
        extra = jnp.where(
            layer == 0,
            first,
            jnp.where(layer == 1, second, jnp.where(layer == depth - 1, last, jnp.where(layer == depth - 2, last_but, 0.0))),
        )
        resid[m] = resid[m] + extra * keep

    for g in range(groups):
        lanes = slice(g * LANES, (g + 1) * LANES)
        for m in range(nf):
            mixed = mix(left_ref, resid, m, g)
            work[1, m, 0:2, lanes] = mixed[0:2, :]
            work[1, m, 2:4, lanes] = mixed[depth - 2 :, :]
    for message in (1, 2, 4):
        send_message(message)
    keep_part(1)

    def fringe_left(i, _):
        fringe_copy(i, me_b, me_b).wait_send()
        return 0

    lax.fori_loop(0, n_blk - 1, fringe_left, 0)

    @pl.when(me_p < n_pen - 1)
    def _():
        upward.wait_send()

    @pl.when(me_p > 0)
    def _():
        downward.wait_send()

    loaded("linv", "right")

    def back_copy(f, peer, half, g):
        field = 4 if f == 2 else half * 2 + f
        return pltpu.make_async_remote_copy(
            src_ref=solved_line.at[f, slab_rows(peer), :],
            dst_ref=solved.at[field, :, lane_group(g)],
            send_sem=back_send.at[f, peer],
            recv_sem=back_recv.at[f, half * n_a + g],
            device_id={"pen": peer},
            device_id_type=MESH,
        )

    def solve(f):
        field = 4 if f == 2 else zh * 2 + f

        def arrive(half, g):
            for message in ((0, 1), (2,), (3, 4))[f]:
                fwd_copy(message, half, g, half * n_a + g).wait_recv()
            return 0

        each_source(arrive)
        for p in range(n_pen):
            work_line[p * depth : p * depth + 2, :] = parts_in[1, f, p, 0:2, :]
            work_line[p * depth + 2 : p * depth + 6, :] = parts_in[0, f, p]
            work_line[p * depth + 6 : (p + 1) * depth, :] = parts_in[1, f, p, 2:4, :]
        solved_line[f] = jnp.dot(
            linv_ref[field], work_line[...], precision=lax.Precision.HIGHEST, preferred_element_type=f32
        )

        def send(half, g):
            back_copy(f, half * n_a + g, zh, a).start()
            return 0

        each_peer(send)
        solved[field, :, lane_group(a)] = solved_line[f, slab_rows(me_p), :]

    solve(0)
    solve(1)

    @pl.when(third)
    def _():
        solve(2)

    def fwd_left(half, g):
        for message in range(3):
            fwd_copy(message, half, g, me_p).wait_send()

        @pl.when(takes_third(half, g))
        def _():
            for message in (3, 4):
                fwd_copy(message, half, g, me_p).wait_send()

        return 0

    each_peer(fwd_left)

    def back_left(half, g):
        for f in range(2):
            back_copy(f, half * n_a + g, zh, a).wait_send()

        @pl.when(third)
        def _():
            back_copy(2, half * n_a + g, zh, a).wait_send()

        return 0

    each_peer(back_left)

    def recv_back(half, g):
        for f in range(2):
            back_copy(f, half * n_a + g, half, g).wait_recv()

        @pl.when(takes_third(half, g))
        def _():
            back_copy(2, half * n_a + g, half, g).wait_recv()

        return 0

    each_source(recv_back)

    for g in range(groups):
        lanes = slice(g * LANES, (g + 1) * LANES)
        for m in range(nf):
            out_ref[m, :, lanes] = filled[m, :, lanes] + keep[:, lanes] * mix(right_ref, solved, m, g)


def solution(mesh):
    n_blk, n_pen = mesh.shape["blk"], mesh.shape["pen"]

    def shards(
        state,
        previous,
        iblank,
        block_owner,
        donor_cell,
        donor_weight,
        send_count,
        recv_cell,
        speed,
        left_vectors,
        right_vectors,
        line_inverse,
    ):
        _, depth, nf, pencils = state.shape
        groups = pencils // LANES
        points = line_inverse.shape[-1]
        cap, donors = recv_cell.shape[-1], donor_cell.shape[-1]
        f32 = jnp.float32
        hbm = pl.BlockSpec(memory_space=pltpu.HBM)
        vmem = pl.BlockSpec(memory_space=pltpu.VMEM)
        dma = pltpu.SemaphoreType.DMA
        out = pl.pallas_call(
            functools.partial(kernel, n_blk, n_pen),
            out_shape=jax.ShapeDtypeStruct((nf, depth, pencils), f32),
            in_specs=[hbm] * 12,
            out_specs=vmem,
            scratch_shapes=[
                pltpu.SMEM((n_blk,), jnp.int32),
                pltpu.SMEM((n_blk,), jnp.int32),
                pltpu.VMEM((nf, depth, pencils), f32),
                pltpu.VMEM((nf, depth, pencils), f32),
                pltpu.VMEM((depth, pencils), jnp.int32),
                pltpu.VMEM((n_blk, donors, cap), jnp.int32),
                pltpu.VMEM((n_blk, donors, cap), f32),
                pltpu.VMEM((n_blk, cap), jnp.int32),
                pltpu.VMEM((nf * groups, LANES), f32),
                pltpu.VMEM((nf * nf * groups, LANES), f32),
                pltpu.VMEM((nf * nf * groups, LANES), f32),
                pltpu.VMEM((nf, points, points), f32),
                dma((12,)),
                pltpu.VMEM((1, LANES), jnp.int32),
                pltpu.SMEM((1, LANES), jnp.int32),
                dma(()),
                pltpu.VMEM((2, groups * depth, LANES), jnp.int32),
                pltpu.VMEM((n_blk, nf, cap), f32),
                pltpu.VMEM((n_blk, nf, cap), f32),
                pltpu.VMEM((nf, depth, pencils), f32),
                pltpu.VMEM((2, nf, 2, pencils), f32),
                pltpu.VMEM((2, nf, 2, pencils), f32),
                pltpu.VMEM((nf, depth, pencils), f32),
                pltpu.VMEM((2, nf, depth // 2, pencils), f32),
                pltpu.VMEM((2, 3, n_pen, depth // 2, LANES), f32),
                pltpu.VMEM((points, LANES), f32),
                pltpu.VMEM((3, points, LANES), f32),
                pltpu.VMEM((nf, depth, pencils), f32),
                dma((n_blk,)),
                dma((n_blk,)),
                dma((2,)),
                dma((2,)),
                dma((5, n_pen)),
                dma((5, n_pen)),
                dma((3, n_pen)),
                dma((3, n_pen)),
            ],
            compiler_params=pltpu.CompilerParams(
                collective_id=0, has_side_effects=True, vmem_limit_bytes=60 * 1024 * 1024
            ),
        )(
            block_owner,
            send_count.reshape(n_blk),
            state[0].transpose(1, 0, 2),
            previous[0].transpose(1, 0, 2),
            iblank[0],
            donor_cell[0, 0].transpose(0, 2, 1),
            donor_weight[0, 0].transpose(0, 2, 1),
            recv_cell[0, 0],
            speed.reshape(nf * groups, LANES),
            left_vectors.reshape(nf * nf * groups, LANES),
            right_vectors.reshape(nf * nf * groups, LANES),
            line_inverse[0],
        )
        return out.transpose(1, 0, 2)[None]

    placed = (
        P("blk", "pen", None, None),
        P("blk", "pen", None, None),
        P("blk", "pen", None),
        P(),
        P("pen", "blk", None, None, None),
        P("pen", "blk", None, None, None),
        P("pen", "blk", None),
        P("pen", "blk", None, None),
        P("blk", None, None),
        P("blk", None, None, None),
        P("blk", None, None, None),
        P("blk", None, None, None),
    )
    return jax.shard_map(
        shards, mesh=mesh, in_specs=placed, out_specs=P("blk", "pen", None, None), check_vma=False
    )
```

time: 1380 us -> 94.9 us (0.07)
  the two profiles are of different devices: /device:TPU:97 before, /device:TPU:1 now
where the time goes in v1:
time: 94.9 us; the launch traced here: 94.8 us
  Pallas kernels  93.2 us (98%)
  local copies, waits for them, and re-layouts  1.59 us (2%)
    pallas_call x1, Pallas kernels, shards(): pl.pallas_call(functools.partial(kernel, n_blk, n_pen), out_shape=jax.Sha...  93.2 us

profile of v1, /device:TPU:1, one launch (start us, length us, event | category | flops | bytes accessed | tf_op | source)
XLA Modules:
  0.0 94.8 jit_solution(14863516343497890340)
XLA Ops:
  0.0 93.2 %shard_map.118 = f32[5,8,1024]{2,1,0:T(8,128)} custom-call(s32[32]{0:T(128)} %owner_hbm.1, s32[32]{0:T(128)} %bitcast.33, f32[5,8,1024]{2,1,0:T(8,128)} %bitcast.24, f32[5,8,1024]{2,1,0:T(8,128)} %bitcast.25, s32[8,1024]{1,0:T(8,128)} %bitcast.30, s32[32,8,128]{2,1,0:T(8,128)} %bitcast.26, f32[32,8,128]{2,1,0:T(8,128)} %bitcast.27, s32[32,128]{1,0:T(8,128)} %bitcast.32, ...), custom_call_target="tpu_custom_call" | custom-call | tf_op jit(solution)/shard_map/pallas_call | solution.py:520
  93.2 1.6 %copy.14 = f32[1,8,5,1024]{3,1,2,0:T(8,128)} copy(f32[1,8,5,1024]{3,1,2,0:T(8,128)} %bitcast.22) | data formatting | bytes 327680

commit v2 on v1

v2 whole, which is shorter than its diff:
```python
import functools

import jax
import jax.numpy as jnp
from jax import lax
from jax.experimental import pallas as pl
from jax.experimental.pallas import tpu as pltpu
from jax.sharding import PartitionSpec as P

MESH = pl.DeviceIdType.MESH
LANES = 128
DEAD = 1e30
WIDE = 256
TOGETHER = 2
PLACED = 4


def split(value):
    high = value.astype(jnp.bfloat16)
    return high, (value - high.astype(jnp.float32)).astype(jnp.bfloat16)


def log2(n):
    assert n & (n - 1) == 0
    return n.bit_length() - 1


def kernel(
    n_blk,
    n_pen,
    owner_hbm,
    count_hbm,
    state_hbm,
    prev_hbm,
    iblank_hbm,
    dcell_hbm,
    dweight_hbm,
    rcell_hbm,
    speed_hbm,
    left_hbm,
    right_hbm,
    linv_hbm,
    out_ref,
    owner_ref,
    count_ref,
    state_ref,
    prev_ref,
    iblank_ref,
    dcell_ref,
    dweight_ref,
    rcell_ref,
    speed_ref,
    left_ref,
    right_ref,
    linv_ref,
    load_sem,
    held_vec,
    held_ref,
    held_sem,
    lo_iota,
    recv_lanes,
    parts,
    placed,
    rows_out,
    rows_in,
    filled,
    halo_out,
    halo_in,
    resid,
    work,
    parts_in,
    work_line,
    solved_line,
    solved,
    linv_in,
    linv_send,
    linv_recv,
    fringe_send,
    fringe_recv,
    halo_send,
    halo_recv,
    fwd_send,
    fwd_recv,
    back_send,
    back_recv,
):
    nf, depth, pencils = state_hbm.shape
    groups = pencils // LANES
    n_a = n_pen // 2
    assert n_a == groups and depth == 8 and nf == 5
    wides = pencils // WIDE
    n_hi = wides * depth
    p_bits, w_bits = log2(pencils), log2(WIDE)
    f32, i32 = jnp.float32, jnp.int32

    me_b = lax.axis_index("blk")
    me_p = lax.axis_index("pen")
    zh = lax.div(me_p, n_a)
    a = lax.rem(me_p, n_a)
    third = lax.rem(a, 2) == zh

    def lane_group(g):
        return pl.ds(pl.multiple_of(g * LANES, LANES), LANES)

    @pl.when(me_p == 0)
    def _():
        halo_in[0] = jnp.zeros(halo_in.shape[1:], f32)

    @pl.when(me_p == n_pen - 1)
    def _():
        halo_in[1] = jnp.zeros(halo_in.shape[1:], f32)

    barrier = pltpu.get_barrier_semaphore()

    partner = lax.rem(me_b + n_blk // 2, n_blk)

    def greet(where):
        pl.semaphore_signal(barrier, inc=1, device_id=where, device_id_type=MESH)

    def greet_blk(off, _):
        greet({"blk": lax.rem(me_b + off, n_blk)})
        return 0

    def greet_lines(off, _):
        greet({"blk": partner, "pen": lax.rem(me_p + off, n_pen)})
        return 0

    lax.fori_loop(1, n_blk, greet_blk, 0)
    lax.fori_loop(1, n_pen, greet_lines, 0)

    greet({"pen": lax.rem(me_p + 1, n_pen)})
    greet({"pen": lax.rem(me_p + n_pen - 1, n_pen)})

    def met():
        pl.semaphore_wait(barrier, n_blk - 1 + n_pen - 1 + 2)

    loads = {}
    for name, source, target in (
        ("rcell", rcell_hbm, rcell_ref),
        ("owner", owner_hbm, owner_ref),
        ("count", count_hbm, count_ref),
        ("state", state_hbm, state_ref),
        ("dcell", dcell_hbm, dcell_ref),
        ("dweight", dweight_hbm, dweight_ref),
        ("prev", prev_hbm, prev_ref),
        ("iblank", iblank_hbm, iblank_ref),
        ("speed", speed_hbm, speed_ref),
        ("left", left_hbm, left_ref),
        ("linv", linv_hbm, linv_ref),
        ("right", right_hbm, right_ref),
    ):
        loads[name] = pltpu.make_async_copy(source, target, load_sem.at[len(loads)])
        loads[name].start()

    def loaded(*names):
        for name in names:
            loads[name].wait()

    lane = lax.broadcasted_iota(i32, (1, LANES), 1)
    lo_iota[...] = lax.broadcasted_iota(i32, (WIDE, LANES), 0).astype(f32).astype(jnp.bfloat16)

    def high_of(cells):
        wide = lax.shift_right_logical(cells, w_bits) & (wides - 1)
        return wide * depth + lax.shift_right_logical(cells, p_bits)

    def pick_lanes(cells):
        low = (cells & (WIDE - 1)).astype(f32).astype(jnp.bfloat16)
        return jnp.where(lo_iota[...] == low, jnp.bfloat16(1), jnp.bfloat16(0))

    loaded("owner")
    held = jnp.zeros((1, LANES), i32)
    for b in range(n_blk):
        held = jnp.where(lane == owner_ref[b], b, held)
    held_vec[...] = held
    held_copy = pltpu.make_async_copy(held_vec, held_ref, held_sem)
    held_copy.start()

    held_copy.wait()

    loaded("count", "state", "dcell", "dweight")
    tiles = [state_ref[m, :, w * WIDE : (w + 1) * WIDE] for m in range(nf) for w in range(wides)]
    n_rows = nf * n_hi
    parts[...] = jnp.concatenate(split(jnp.concatenate(tiles, axis=0)), axis=0)

    def fringe_offset(i):
        return n_blk // 2 + lax.div(i + 1, 2) * (2 * lax.rem(i, 2) - 1)

    def fringe_copy(slot, peer, source):
        return pltpu.make_async_remote_copy(
            src_ref=rows_out.at[slot],
            dst_ref=rows_in.at[source],
            send_sem=fringe_send.at[slot],
            recv_sem=fringe_recv.at[source],
            device_id={"blk": peer},
            device_id_type=MESH,
        )

    hi_iota = lax.broadcasted_iota(i32, (n_hi, LANES), 0)
    donors = dcell_ref.shape[1]

    def interpolate(q, send):
        for u in range(TOGETHER):
            slot = q * TOGETHER + u
            peer = lax.rem(me_b + fringe_offset(slot), n_blk)
            block = held_ref[0, peer]
            cells, weights = dcell_ref[block], dweight_ref[block]
            acc = [None] * nf
            for i in range(0, donors, 2):
                pair = [cells[k : k + 1, :] for k in (i, i + 1)]
                picks = jnp.concatenate([pick_lanes(c) for c in pair], axis=1)
                both = jnp.dot(parts[...], picks, preferred_element_type=f32)
                both = both[:n_rows] + both[n_rows:]
                for k in range(2):
                    weight = jnp.where(hi_iota == high_of(pair[k]), weights[i + k : i + k + 1, :], 0.0)
                    for m in range(nf):
                        term = both[m * n_hi : (m + 1) * n_hi, k * LANES : (k + 1) * LANES] * weight
                        term = sum(term[w * depth : (w + 1) * depth] for w in range(wides))
                        acc[m] = term if acc[m] is None else acc[m] + term
            live = lane < count_ref[block]
            for m in range(nf):
                row = jnp.sum(acc[m], axis=0, keepdims=True)
                if m == 0:
                    row = jnp.where(live, row, DEAD)
                rows_out[slot, pl.ds(m, 1), :] = row

            if send:

                @pl.when(slot < n_blk - 1)
                def _():
                    fringe_copy(slot, peer, me_b).start()

        return 0

    def send_ready(slot, _):
        fringe_copy(slot, lax.rem(me_b + fringe_offset(slot), n_blk), me_b).start()
        return 0

    def inverse_copies():
        def copy(i, field, count):
            return pltpu.make_async_remote_copy(
                src_ref=linv_ref.at[pl.ds(field, count)],
                dst_ref=linv_in.at[pl.ds(2 * i, count)],
                send_sem=linv_send.at[i],
                recv_sem=linv_recv.at[i],
                device_id={"blk": partner},
                device_id_type=MESH,
            )

        return copy(0, zh * 2, 2), copy(1, 4, 1)

    steps = n_blk // TOGETHER
    lax.fori_loop(0, steps // 2, lambda q, _: interpolate(q, False), 0)
    met()
    lax.fori_loop(0, steps // 2 * TOGETHER, send_ready, 0)
    loaded("linv")
    inverses = inverse_copies()
    inverses[0].start()

    @pl.when(third)
    def _():
        inverses[1].start()

    lax.fori_loop(steps // 2, steps, lambda q, _: interpolate(q, True), 0)

    loaded("rcell")

    def receivers(b, _):
        recv_lanes[b] = pick_lanes(rcell_ref[pl.ds(b, 1), :])
        return 0

    lax.fori_loop(0, n_blk, receivers, 0)
    rows_in[me_b] = jnp.full(rows_in.shape[1:], DEAD, f32)

    placed[...] = jnp.zeros_like(placed)

    def place(q, _):
        tall, flat = [], []
        for u in range(PLACED):
            i = q * PLACED + u
            source = lax.rem(me_b - fringe_offset(i) + n_blk, n_blk)

            @pl.when(i < n_blk - 1)
            def _():
                fringe_copy(i, source, source).wait_recv()

            block = held_ref[0, source]
            rows = [rows_in[source, m : m + 1, :] for m in range(nf)]
            here = (hi_iota == high_of(rcell_ref[pl.ds(block, 1), :])) & (rows[0] < 0.5 * DEAD)
            high, low = split(jnp.concatenate([jnp.where(here, row, 0.0) for row in rows], axis=0))
            hit = jnp.where(here, 1.0, 0.0).astype(jnp.bfloat16)
            tall.append(jnp.concatenate([high, low, hit], axis=0))
            flat.append(recv_lanes[block])
        placed[...] += lax.dot_general(
            jnp.concatenate(tall, axis=1),
            jnp.concatenate(flat, axis=1),
            (((1,), (1,)), ((), ())),
            preferred_element_type=f32,
        )
        return 0

    lax.fori_loop(0, n_blk // PLACED, place, 0)
    for m in range(nf):
        for w in range(wides):
            at, lanes = m * n_hi + w * depth, slice(w * WIDE, (w + 1) * WIDE)
            value = placed[at : at + depth, :] + placed[n_rows + at : n_rows + at + depth, :]
            hit = placed[2 * n_rows + w * depth : 2 * n_rows + (w + 1) * depth, :]
            filled[m, :, lanes] = jnp.where(hit > 0.5, value, state_ref[m, :, lanes])

    def halo_copy(way, peer):
        return pltpu.make_async_remote_copy(
            src_ref=halo_out.at[way],
            dst_ref=halo_in.at[way],
            send_sem=halo_send.at[way],
            recv_sem=halo_recv.at[way],
            device_id={"pen": peer},
            device_id_type=MESH,
        )

    halo_out[0] = filled[:, depth - 2 :, :]
    halo_out[1] = filled[:, :2, :]
    upward = halo_copy(0, lax.rem(me_p + 1, n_pen))
    downward = halo_copy(1, lax.rem(me_p + n_pen - 1, n_pen))

    @pl.when(me_p < n_pen - 1)
    def _():
        upward.start()

    @pl.when(me_p > 0)
    def _():
        downward.start()

    loaded("prev", "iblank", "speed", "left")
    layer = lax.broadcasted_iota(i32, (depth, pencils), 0)
    keep = iblank_ref[...].astype(f32)

    def wave(m):
        return jnp.concatenate([speed_ref[m * groups + g : m * groups + g + 1, :] for g in range(groups)], axis=1)

    for m in range(nf):
        cur = filled[m]
        upper = jnp.where(layer == depth - 1, 0.0, pltpu.roll(cur, depth - 1, 0))
        upper_two = jnp.where(layer >= depth - 2, 0.0, pltpu.roll(cur, depth - 2, 0))
        lower = jnp.where(layer == 0, 0.0, pltpu.roll(cur, 1, 0))
        lower_two = jnp.where(layer <= 1, 0.0, pltpu.roll(cur, 2, 0))
        r = -(cur - prev_ref[m]) - 0.5 * wave(m) * (upper - lower)
        r = r + 0.25 * (upper - 2.0 * cur + lower)
        r = r - 0.0625 * (upper_two - 4.0 * upper + 6.0 * cur - 4.0 * lower + lower_two)
        r = r - 0.25 * (pltpu.roll(cur, pencils - 1, 1) - pltpu.roll(cur, 1, 1))
        resid[m] = r * keep

    def mix(matrix_ref, value, m, g):
        total = None
        for n in range(nf):
            at = (m * nf + n) * groups + g
            term = matrix_ref[at : at + 1, :] * value(n, g)
            total = term if total is None else total + term
        return total

    def resid_at(n, g):
        return resid[n, :, g * LANES : (g + 1) * LANES]

    def place_of(m, g):
        return (g % 2, g, 2) if m == 4 else (m // 2, g, m % 2)

    def each_peer(do):
        lax.fori_loop(0, n_a, lambda i, _: do(1 - zh, lax.rem(a + i, n_a)), 0)
        lax.fori_loop(0, n_a, lambda i, _: do(zh, lax.rem(a + i, n_a)), 0)

    def each_source(do):
        lax.fori_loop(0, n_a, lambda i, _: do(zh, lax.rem(a + n_a - i, n_a)), 0)
        lax.fori_loop(0, n_a, lambda i, _: do(1 - zh, lax.rem(a + n_a - i, n_a)), 0)

    def takes_third(half, g):
        return lax.rem(g, 2) == half

    def sized(more, do):
        @pl.when(more)
        def _():
            do(3)

        @pl.when(jnp.logical_not(more))
        def _():
            do(2)

        return 0

    def fwd_copy(part, half, g, source, count):
        peer = half * n_a + g
        return pltpu.make_async_remote_copy(
            src_ref=work.at[part, half, g, pl.ds(0, count)],
            dst_ref=parts_in.at[part, source, pl.ds(0, count)],
            send_sem=fwd_send.at[part, peer],
            recv_sem=fwd_recv.at[part, source],
            device_id={"blk": partner, "pen": peer},
            device_id_type=MESH,
        )

    def send_part(part):
        each_peer(
            lambda half, g: sized(
                takes_third(half, g), lambda count: fwd_copy(part, half, g, me_p, count).start()
            )
        )

    for g in range(groups):
        for m in range(nf):
            work[(0, *place_of(m, g))] = mix(left_ref, resid_at, m, g)[2 : depth - 2, :]
    send_part(0)

    @pl.when(me_p > 0)
    def _():
        upward.wait_recv()

    @pl.when(me_p < n_pen - 1)
    def _():
        downward.wait_recv()

    for m in range(nf):
        low2, low1 = halo_in[0, m, 0:1, :], halo_in[0, m, 1:2, :]
        up1, up2 = halo_in[1, m, 0:1, :], halo_in[1, m, 1:2, :]
        speed = wave(m)
        first = (0.5 + 0.5 * speed) * low1 - 0.0625 * low2
        last = (0.5 - 0.5 * speed) * up1 - 0.0625 * up2
        second, last_but = -0.0625 * low1, -0.0625 * up1
        extra = jnp.where(
            layer == 0,
            first,
            jnp.where(layer == 1, second, jnp.where(layer == depth - 1, last, jnp.where(layer == depth - 2, last_but, 0.0))),
        )
        resid[m] = resid[m] + extra * keep

    for g in range(groups):
        for m in range(nf):
            half, at, f = place_of(m, g)
            mixed = mix(left_ref, resid_at, m, g)
            work[1, half, at, f, 0:2, :] = mixed[0:2, :]
            work[1, half, at, f, 2:4, :] = mixed[depth - 2 :, :]
    send_part(1)

    def fringe_left(i, _):
        fringe_copy(i, me_b, me_b).wait_send()
        return 0

    lax.fori_loop(0, n_blk - 1, fringe_left, 0)

    @pl.when(me_p < n_pen - 1)
    def _():
        upward.wait_send()

    @pl.when(me_p > 0)
    def _():
        downward.wait_send()

    loaded("right")
    inverses[0].wait_recv()

    @pl.when(third)
    def _():
        inverses[1].wait_recv()

    def arrive(half, g):
        source = half * n_a + g
        for part in range(2):
            sized(third, lambda count: fwd_copy(part, half, g, source, count).wait_recv())
        return 0

    each_source(arrive)

    def solve(f):
        for p in range(n_pen):
            work_line[p * depth : p * depth + 2, :] = parts_in[1, p, f, 0:2, :]
            work_line[p * depth + 2 : p * depth + 6, :] = parts_in[0, p, f]
            work_line[p * depth + 6 : (p + 1) * depth, :] = parts_in[1, p, f, 2:4, :]
        inv_high, inv_low = split(linv_in[f])
        line_high, line_low = split(work_line[...])
        line = jnp.dot(
            jnp.concatenate([inv_high, inv_high, inv_low], axis=1),
            jnp.concatenate([line_high, line_low, line_high], axis=0),
            preferred_element_type=f32,
        )
        for p in range(n_pen):
            solved_line[p, f] = line[p * depth : (p + 1) * depth, :]

    solve(0)
    solve(1)

    @pl.when(third)
    def _():
        solve(2)

    def back_copy(peer, half, g, count):
        return pltpu.make_async_remote_copy(
            src_ref=solved_line.at[peer, pl.ds(0, count)],
            dst_ref=solved.at[half, g, pl.ds(0, count)],
            send_sem=back_send.at[peer],
            recv_sem=back_recv.at[half * n_a + g],
            device_id={"blk": partner, "pen": peer},
            device_id_type=MESH,
        )

    each_peer(
        lambda half, g: sized(third, lambda count: back_copy(half * n_a + g, zh, a, count).start())
    )

    inverses[0].wait_send()

    @pl.when(third)
    def _():
        inverses[1].wait_send()

    def left(half, g):
        for part in range(2):
            sized(takes_third(half, g), lambda count: fwd_copy(part, half, g, me_p, count).wait_send())
        return sized(third, lambda count: back_copy(half * n_a + g, zh, a, count).wait_send())

    each_peer(left)
    each_source(
        lambda half, g: sized(
            takes_third(half, g), lambda count: back_copy(half * n_a + g, half, g, count).wait_recv()
        )
    )

    def solved_at(n, g):
        return solved[place_of(n, g)]

    for g in range(groups):
        lanes = slice(g * LANES, (g + 1) * LANES)
        for m in range(nf):
            out_ref[m, :, lanes] = filled[m, :, lanes] + keep[:, lanes] * mix(right_ref, solved_at, m, g)


def solution(mesh):
    n_blk, n_pen = mesh.shape["blk"], mesh.shape["pen"]

    def shards(
        state,
        previous,
        iblank,
        block_owner,
        donor_cell,
        donor_weight,
        send_count,
        recv_cell,
        speed,
        left_vectors,
        right_vectors,
        line_inverse,
    ):
        _, depth, nf, pencils = state.shape
        groups, n_hi = pencils // LANES, pencils // WIDE * depth
        points = line_inverse.shape[-1]
        cap, donors = recv_cell.shape[-1], donor_cell.shape[-1]
        f32 = jnp.float32
        hbm = pl.BlockSpec(memory_space=pltpu.HBM)
        vmem = pl.BlockSpec(memory_space=pltpu.VMEM)
        dma = pltpu.SemaphoreType.DMA
        out = pl.pallas_call(
            functools.partial(kernel, n_blk, n_pen),
            out_shape=jax.ShapeDtypeStruct((nf, depth, pencils), f32),
            in_specs=[hbm] * 12,
            out_specs=vmem,
            scratch_shapes=[
                pltpu.SMEM((n_blk,), jnp.int32),
                pltpu.SMEM((n_blk,), jnp.int32),
                pltpu.VMEM((nf, depth, pencils), f32),
                pltpu.VMEM((nf, depth, pencils), f32),
                pltpu.VMEM((depth, pencils), jnp.int32),
                pltpu.VMEM((n_blk, donors, cap), jnp.int32),
                pltpu.VMEM((n_blk, donors, cap), f32),
                pltpu.VMEM((n_blk, cap), jnp.int32),
                pltpu.VMEM((nf * groups, LANES), f32),
                pltpu.VMEM((nf * nf * groups, LANES), f32),
                pltpu.VMEM((nf * nf * groups, LANES), f32),
                pltpu.VMEM((nf, points, points), f32),
                dma((12,)),
                pltpu.VMEM((1, LANES), jnp.int32),
                pltpu.SMEM((1, LANES), jnp.int32),
                dma(()),
                pltpu.VMEM((WIDE, LANES), jnp.bfloat16),
                pltpu.VMEM((n_blk, WIDE, LANES), jnp.bfloat16),
                pltpu.VMEM((2 * nf * n_hi, WIDE), jnp.bfloat16),
                pltpu.VMEM(((2 * nf + 1) * n_hi, WIDE), f32),
                pltpu.VMEM((n_blk, nf, cap), f32),
                pltpu.VMEM((n_blk, nf, cap), f32),
                pltpu.VMEM((nf, depth, pencils), f32),
                pltpu.VMEM((2, nf, 2, pencils), f32),
                pltpu.VMEM((2, nf, 2, pencils), f32),
                pltpu.VMEM((nf, depth, pencils), f32),
                pltpu.VMEM((2, 2, groups, 3, depth // 2, LANES), f32),
                pltpu.VMEM((2, n_pen, 3, depth // 2, LANES), f32),
                pltpu.VMEM((points, LANES), f32),
                pltpu.VMEM((n_pen, 3, depth, LANES), f32),
                pltpu.VMEM((2, groups, 3, depth, LANES), f32),
                pltpu.VMEM((3, points, points), f32),
                dma((2,)),
                dma((2,)),
                dma((n_blk,)),
                dma((n_blk,)),
                dma((2,)),
                dma((2,)),
                dma((2, n_pen)),
                dma((2, n_pen)),
                dma((n_pen,)),
                dma((n_pen,)),
            ],
            compiler_params=pltpu.CompilerParams(
                collective_id=0, has_side_effects=True, vmem_limit_bytes=60 * 1024 * 1024
            ),
        )(
            block_owner,
            send_count.reshape(n_blk),
            state[0].transpose(1, 0, 2),
            previous[0].transpose(1, 0, 2),
            iblank[0],
            donor_cell[0, 0].transpose(0, 2, 1),
            donor_weight[0, 0].transpose(0, 2, 1),
            recv_cell[0, 0],
            speed.reshape(nf * groups, LANES),
            left_vectors.reshape(nf * nf * groups, LANES),
            right_vectors.reshape(nf * nf * groups, LANES),
            line_inverse[0],
        )
        return out.transpose(1, 0, 2)[None]

    placed = (
        P("blk", "pen", None, None),
        P("blk", "pen", None, None),
        P("blk", "pen", None),
        P(),
        P("pen", "blk", None, None, None),
        P("pen", "blk", None, None, None),
        P("pen", "blk", None),
        P("pen", "blk", None, None),
        P("blk", None, None),
        P("blk", None, None, None),
        P("blk", None, None, None),
        P("blk", None, None, None),
    )
    return jax.shard_map(
        shards, mesh=mesh, in_specs=placed, out_specs=P("blk", "pen", None, None), check_vma=False
    )
```

time: 94.9 us -> 70.4 us (0.74)
  the two profiles are of different devices: /device:TPU:1 before, /device:TPU:69 now
where the time goes in v2:
time: 70.4 us; the launch traced here: 70.2 us
  Pallas kernels  68.6 us (97%)
  local copies, waits for them, and re-layouts  1.59 us (2%)
    pallas_call x1, Pallas kernels, shards(): pl.pallas_call(functools.partial(kernel, n_blk, n_pen), out_shape=jax.Sha...  68.6 us
    unnamed x1, local copies, waits for them, and re-layouts  1.59 us

profile of v2, /device:TPU:69, one launch (start us, length us, event | category | flops | bytes accessed | tf_op | source)
XLA Modules:
  0.0 70.2 jit_solution(15631214588673404039)
XLA Ops:
  0.0 68.6 %shard_map.118 = f32[5,8,1024]{2,1,0:T(8,128)} custom-call(s32[32]{0:T(128)} %owner_hbm.1, s32[32]{0:T(128)} %bitcast.33, f32[5,8,1024]{2,1,0:T(8,128)} %bitcast.24, f32[5,8,1024]{2,1,0:T(8,128)} %bitcast.25, s32[8,1024]{1,0:T(8,128)} %bitcast.30, s32[32,8,128]{2,1,0:T(8,128)} %bitcast.26, f32[32,8,128]{2,1,0:T(8,128)} %bitcast.27, s32[32,128]{1,0:T(8,128)} %bitcast.32, ...), custom_call_target="tpu_custom_call" | custom-call | tf_op jit(solution)/shard_map/pallas_call | solution.py:557
  68.6 1.6 %copy.14 = f32[1,8,5,1024]{3,1,2,0:T(8,128)} copy(f32[1,8,5,1024]{3,1,2,0:T(8,128)} %bitcast.22) | data formatting | bytes 327680

commit v3 on v2

--- a/solution.py
+++ b/solution.py
@@ -11,7 +11,7 @@
 LANES = 128
 DEAD = 1e30
 WIDE = 256
-TOGETHER = 2
+TOGETHER = 4
 PLACED = 4
 
 
@@ -72,9 +72,6 @@
     work_line,
     solved_line,
     solved,
-    linv_in,
-    linv_send,
-    linv_recv,
     fringe_send,
     fringe_recv,
     halo_send,
@@ -102,46 +99,14 @@
     def lane_group(g):
         return pl.ds(pl.multiple_of(g * LANES, LANES), LANES)
 
-    @pl.when(me_p == 0)
-    def _():
-        halo_in[0] = jnp.zeros(halo_in.shape[1:], f32)
-
-    @pl.when(me_p == n_pen - 1)
-    def _():
-        halo_in[1] = jnp.zeros(halo_in.shape[1:], f32)
-
-    barrier = pltpu.get_barrier_semaphore()
-
-    partner = lax.rem(me_b + n_blk // 2, n_blk)
-
-    def greet(where):
-        pl.semaphore_signal(barrier, inc=1, device_id=where, device_id_type=MESH)
-
-    def greet_blk(off, _):
-        greet({"blk": lax.rem(me_b + off, n_blk)})
-        return 0
-
-    def greet_lines(off, _):
-        greet({"blk": partner, "pen": lax.rem(me_p + off, n_pen)})
-        return 0
-
-    lax.fori_loop(1, n_blk, greet_blk, 0)
-    lax.fori_loop(1, n_pen, greet_lines, 0)
-
-    greet({"pen": lax.rem(me_p + 1, n_pen)})
-    greet({"pen": lax.rem(me_p + n_pen - 1, n_pen)})
-
-    def met():
-        pl.semaphore_wait(barrier, n_blk - 1 + n_pen - 1 + 2)
-
     loads = {}
     for name, source, target in (
-        ("rcell", rcell_hbm, rcell_ref),
         ("owner", owner_hbm, owner_ref),
-        ("count", count_hbm, count_ref),
         ("state", state_hbm, state_ref),
         ("dcell", dcell_hbm, dcell_ref),
         ("dweight", dweight_hbm, dweight_ref),
+        ("count", count_hbm, count_ref),
+        ("rcell", rcell_hbm, rcell_ref),
         ("prev", prev_hbm, prev_ref),
         ("iblank", iblank_hbm, iblank_ref),
         ("speed", speed_hbm, speed_ref),
@@ -155,6 +120,26 @@
     def loaded(*names):
         for name in names:
             loads[name].wait()
+
+    @pl.when(me_p == 0)
+    def _():
+        halo_in[0] = jnp.zeros(halo_in.shape[1:], f32)
+
+    @pl.when(me_p == n_pen - 1)
+    def _():
+        halo_in[1] = jnp.zeros(halo_in.shape[1:], f32)
+
+    barrier = pltpu.get_barrier_semaphore()
+
+    def greet(where):
+        pl.semaphore_signal(barrier, inc=1, device_id=where, device_id_type=MESH)
+        return 0
+
+    lax.fori_loop(1, n_blk, lambda off, _: greet({"blk": lax.rem(me_b + off, n_blk)}), 0)
+    lax.fori_loop(1, n_pen, lambda off, _: greet({"pen": lax.rem(me_p + off, n_pen)}), 0)
+
+    def met():
+        pl.semaphore_wait(barrier, n_blk - 1 + n_pen - 1)
 
     lane = lax.broadcasted_iota(i32, (1, LANES), 1)
     lo_iota[...] = lax.broadcasted_iota(i32, (WIDE, LANES), 0).astype(f32).astype(jnp.bfloat16)
@@ -223,43 +208,25 @@
                     row = jnp.where(live, row, DEAD)
                 rows_out[slot, pl.ds(m, 1), :] = row
 
-            if send:
-
-                @pl.when(slot < n_blk - 1)
-                def _():
-                    fringe_copy(slot, peer, me_b).start()
+        if send:
+            for u in range(TOGETHER - 1):
+                send_ready(q * TOGETHER + u, 0)
+            last = q * TOGETHER + TOGETHER - 1
+
+            @pl.when(last < n_blk - 1)
+            def _():
+                send_ready(last, 0)
 
         return 0
 
     def send_ready(slot, _):
         fringe_copy(slot, lax.rem(me_b + fringe_offset(slot), n_blk), me_b).start()
         return 0
-
-    def inverse_copies():
-        def copy(i, field, count):
-            return pltpu.make_async_remote_copy(
-                src_ref=linv_ref.at[pl.ds(field, count)],
-                dst_ref=linv_in.at[pl.ds(2 * i, count)],
-                send_sem=linv_send.at[i],
-                recv_sem=linv_recv.at[i],
-                device_id={"blk": partner},
-                device_id_type=MESH,
-            )
-
-        return copy(0, zh * 2, 2), copy(1, 4, 1)
 
     steps = n_blk // TOGETHER
     lax.fori_loop(0, steps // 2, lambda q, _: interpolate(q, False), 0)
     met()
     lax.fori_loop(0, steps // 2 * TOGETHER, send_ready, 0)
-    loaded("linv")
-    inverses = inverse_copies()
-    inverses[0].start()
-
-    @pl.when(third)
-    def _():
-        inverses[1].start()
-
     lax.fori_loop(steps // 2, steps, lambda q, _: interpolate(q, True), 0)
 
     loaded("rcell")
@@ -274,15 +241,17 @@
     placed[...] = jnp.zeros_like(placed)
 
     def place(q, _):
+        sources = [lax.rem(me_b - fringe_offset(q * PLACED + u) + n_blk, n_blk) for u in range(PLACED)]
+        for u in range(PLACED - 1):
+            fringe_copy(q * PLACED + u, sources[u], sources[u]).wait_recv()
+        last = q * PLACED + PLACED - 1
+
+        @pl.when(last < n_blk - 1)
+        def _():
+            fringe_copy(last, sources[-1], sources[-1]).wait_recv()
+
         tall, flat = [], []
-        for u in range(PLACED):
-            i = q * PLACED + u
-            source = lax.rem(me_b - fringe_offset(i) + n_blk, n_blk)
-
-            @pl.when(i < n_blk - 1)
-            def _():
-                fringe_copy(i, source, source).wait_recv()
-
+        for source in sources:
             block = held_ref[0, source]
             rows = [rows_in[source, m : m + 1, :] for m in range(nf)]
             here = (hi_iota == high_of(rcell_ref[pl.ds(block, 1), :])) & (rows[0] < 0.5 * DEAD)
@@ -364,10 +333,10 @@
 
     def each_peer(do):
         lax.fori_loop(0, n_a, lambda i, _: do(1 - zh, lax.rem(a + i, n_a)), 0)
-        lax.fori_loop(0, n_a, lambda i, _: do(zh, lax.rem(a + i, n_a)), 0)
+        lax.fori_loop(1, n_a, lambda i, _: do(zh, lax.rem(a + i, n_a)), 0)
 
     def each_source(do):
-        lax.fori_loop(0, n_a, lambda i, _: do(zh, lax.rem(a + n_a - i, n_a)), 0)
+        lax.fori_loop(1, n_a, lambda i, _: do(zh, lax.rem(a + n_a - i, n_a)), 0)
         lax.fori_loop(0, n_a, lambda i, _: do(1 - zh, lax.rem(a + n_a - i, n_a)), 0)
 
     def takes_third(half, g):
@@ -391,7 +360,7 @@
             dst_ref=parts_in.at[part, source, pl.ds(0, count)],
             send_sem=fwd_send.at[part, peer],
             recv_sem=fwd_recv.at[part, source],
-            device_id={"blk": partner, "pen": peer},
+            device_id={"pen": peer},
             device_id_type=MESH,
         )
 
@@ -401,6 +370,11 @@
                 takes_third(half, g), lambda count: fwd_copy(part, half, g, me_p, count).start()
             )
         )
+
+        def keep_own(count):
+            parts_in[part, me_p, 0:count] = work[part, zh, a, 0:count]
+
+        sized(third, keep_own)
 
     for g in range(groups):
         for m in range(nf):
@@ -451,13 +425,7 @@
     def _():
         downward.wait_send()
 
-    loaded("right")
-    inverses[0].wait_recv()
-
-    @pl.when(third)
-    def _():
-        inverses[1].wait_recv()
-
+    loaded("linv", "right")
     def arrive(half, g):
         source = half * n_a + g
         for part in range(2):
@@ -471,7 +439,7 @@
             work_line[p * depth : p * depth + 2, :] = parts_in[1, p, f, 0:2, :]
             work_line[p * depth + 2 : p * depth + 6, :] = parts_in[0, p, f]
             work_line[p * depth + 6 : (p + 1) * depth, :] = parts_in[1, p, f, 2:4, :]
-        inv_high, inv_low = split(linv_in[f])
+        inv_high, inv_low = split(linv_ref[4 if f == 2 else zh * 2 + f])
         line_high, line_low = split(work_line[...])
         line = jnp.dot(
             jnp.concatenate([inv_high, inv_high, inv_low], axis=1),
@@ -494,7 +462,7 @@
             dst_ref=solved.at[half, g, pl.ds(0, count)],
             send_sem=back_send.at[peer],
             recv_sem=back_recv.at[half * n_a + g],
-            device_id={"blk": partner, "pen": peer},
+            device_id={"pen": peer},
             device_id_type=MESH,
         )
 
@@ -502,11 +470,10 @@
         lambda half, g: sized(third, lambda count: back_copy(half * n_a + g, zh, a, count).start())
     )
 
-    inverses[0].wait_send()
-
-    @pl.when(third)
-    def _():
-        inverses[1].wait_send()
+    def keep_solved(count):
+        solved[zh, a, 0:count] = solved_line[me_p, 0:count]
+
+    sized(third, keep_solved)
 
     def left(half, g):
         for part in range(2):
@@ -591,9 +558,6 @@
                 pltpu.VMEM((points, LANES), f32),
                 pltpu.VMEM((n_pen, 3, depth, LANES), f32),
                 pltpu.VMEM((2, groups, 3, depth, LANES), f32),
-                pltpu.VMEM((3, points, points), f32),
-                dma((2,)),
-                dma((2,)),
                 dma((n_blk,)),
                 dma((n_blk,)),
                 dma((2,)),

time: 70.4 us -> 63 us (0.89)
  the two profiles are of different devices: /device:TPU:69 before, /device:TPU:1 now
where the time goes in v3:
time: 63 us; the launch traced here: 62.9 us
  Pallas kernels  61.3 us (97%)
  local copies, waits for them, and re-layouts  1.59 us (3%)
    pallas_call x1, Pallas kernels, shards(): pl.pallas_call(functools.partial(kernel, n_blk, n_pen), out_shape=jax.Sha...  61.3 us
    unnamed x1, local copies, waits for them, and re-layouts  1.59 us

profile of v3, /device:TPU:1, one launch (start us, length us, event | category | flops | bytes accessed | tf_op | source)
XLA Modules:
  0.0 62.9 jit_solution(12102414084634007616)
XLA Ops:
  0.0 61.3 %shard_map.118 = f32[5,8,1024]{2,1,0:T(8,128)} custom-call(s32[32]{0:T(128)} %owner_hbm.1, s32[32]{0:T(128)} %bitcast.33, f32[5,8,1024]{2,1,0:T(8,128)} %bitcast.24, f32[5,8,1024]{2,1,0:T(8,128)} %bitcast.25, s32[8,1024]{1,0:T(8,128)} %bitcast.30, s32[32,8,128]{2,1,0:T(8,128)} %bitcast.26, f32[32,8,128]{2,1,0:T(8,128)} %bitcast.27, s32[32,128]{1,0:T(8,128)} %bitcast.32, ...), custom_call_target="tpu_custom_call" | custom-call | tf_op jit(solution)/shard_map/pallas_call | solution.py:524
  61.3 1.6 %copy.14 = f32[1,8,5,1024]{3,1,2,0:T(8,128)} copy(f32[1,8,5,1024]{3,1,2,0:T(8,128)} %bitcast.22) | data formatting | bytes 327680

commit v4 on v3

--- a/solution.py
+++ b/solution.py
@@ -183,8 +183,18 @@
     hi_iota = lax.broadcasted_iota(i32, (n_hi, LANES), 0)
     donors = dcell_ref.shape[1]
 
-    def interpolate(q, send):
+    across = lax.broadcasted_iota(i32, (LANES, WIDE), 1).astype(f32)
+
+    def receivers(b):
+        low = (rcell_ref[pl.ds(b, 1), :] & (WIDE - 1)).astype(f32)
+        slots = jnp.broadcast_to(low, (LANES, LANES)).T
+        slots = jnp.concatenate([slots] * (WIDE // LANES), axis=1)
+        recv_lanes[b] = jnp.where(slots == across, 1.0, 0.0).astype(jnp.bfloat16)
+
+    def interpolate(q, send, count):
         for u in range(TOGETHER):
+            receivers(q * TOGETHER + u)
+        for u in range(count):
             slot = q * TOGETHER + u
             peer = lax.rem(me_b + fringe_offset(slot), n_blk)
             block = held_ref[0, peer]
@@ -209,14 +219,8 @@
                 rows_out[slot, pl.ds(m, 1), :] = row
 
         if send:
-            for u in range(TOGETHER - 1):
+            for u in range(count):
                 send_ready(q * TOGETHER + u, 0)
-            last = q * TOGETHER + TOGETHER - 1
-
-            @pl.when(last < n_blk - 1)
-            def _():
-                send_ready(last, 0)
-
         return 0
 
     def send_ready(slot, _):
@@ -224,18 +228,13 @@
         return 0
 
     steps = n_blk // TOGETHER
-    lax.fori_loop(0, steps // 2, lambda q, _: interpolate(q, False), 0)
+    loaded("rcell")
+    lax.fori_loop(0, steps // 2, lambda q, _: interpolate(q, False, TOGETHER), 0)
     met()
     lax.fori_loop(0, steps // 2 * TOGETHER, send_ready, 0)
-    lax.fori_loop(steps // 2, steps, lambda q, _: interpolate(q, True), 0)
-
-    loaded("rcell")
-
-    def receivers(b, _):
-        recv_lanes[b] = pick_lanes(rcell_ref[pl.ds(b, 1), :])
-        return 0
-
-    lax.fori_loop(0, n_blk, receivers, 0)
+    lax.fori_loop(steps // 2, steps - 1, lambda q, _: interpolate(q, True, TOGETHER), 0)
+    interpolate(steps - 1, True, TOGETHER - 1)
+
     rows_in[me_b] = jnp.full(rows_in.shape[1:], DEAD, f32)
 
     placed[...] = jnp.zeros_like(placed)
@@ -259,11 +258,8 @@
             hit = jnp.where(here, 1.0, 0.0).astype(jnp.bfloat16)
             tall.append(jnp.concatenate([high, low, hit], axis=0))
             flat.append(recv_lanes[block])
-        placed[...] += lax.dot_general(
-            jnp.concatenate(tall, axis=1),
-            jnp.concatenate(flat, axis=1),
-            (((1,), (1,)), ((), ())),
-            preferred_element_type=f32,
+        placed[...] += jnp.dot(
+            jnp.concatenate(tall, axis=1), jnp.concatenate(flat, axis=0), preferred_element_type=f32
         )
         return 0
 
@@ -342,44 +338,53 @@
     def takes_third(half, g):
         return lax.rem(g, 2) == half
 
-    def sized(more, do):
+    MESSAGES = ((0, 0, 2), (1, 0, 1), (1, 1, 1))
+    ANSWERS = ((0, 1), (1, 1))
+
+    def sized(first, count, more, do):
+        if first + count < 2:
+            do(count)
+            return 0
+
         @pl.when(more)
         def _():
-            do(3)
+            do(count + 1)
 
         @pl.when(jnp.logical_not(more))
         def _():
-            do(2)
-
-        return 0
-
-    def fwd_copy(part, half, g, source, count):
+            do(count)
+
+        return 0
+
+    def fwd_copy(message, half, g, source, count):
+        part, first, _ = MESSAGES[message]
         peer = half * n_a + g
         return pltpu.make_async_remote_copy(
-            src_ref=work.at[part, half, g, pl.ds(0, count)],
-            dst_ref=parts_in.at[part, source, pl.ds(0, count)],
-            send_sem=fwd_send.at[part, peer],
-            recv_sem=fwd_recv.at[part, source],
+            src_ref=work.at[part, half, g, pl.ds(first, count)],
+            dst_ref=parts_in.at[part, source, pl.ds(first, count)],
+            send_sem=fwd_send.at[message, peer],
+            recv_sem=fwd_recv.at[message, source],
             device_id={"pen": peer},
             device_id_type=MESH,
         )
 
-    def send_part(part):
+    def send_message(message):
+        part, first, count = MESSAGES[message]
         each_peer(
             lambda half, g: sized(
-                takes_third(half, g), lambda count: fwd_copy(part, half, g, me_p, count).start()
+                first, count, takes_third(half, g), lambda n: fwd_copy(message, half, g, me_p, n).start()
             )
         )
 
-        def keep_own(count):
-            parts_in[part, me_p, 0:count] = work[part, zh, a, 0:count]
-
-        sized(third, keep_own)
+        def keep_own(n):
+            parts_in[part, me_p, first : first + n] = work[part, zh, a, first : first + n]
+
+        sized(first, count, third, keep_own)
 
     for g in range(groups):
         for m in range(nf):
             work[(0, *place_of(m, g))] = mix(left_ref, resid_at, m, g)[2 : depth - 2, :]
-    send_part(0)
+    send_message(0)
 
     @pl.when(me_p > 0)
     def _():
@@ -409,7 +414,8 @@
             mixed = mix(left_ref, resid_at, m, g)
             work[1, half, at, f, 0:2, :] = mixed[0:2, :]
             work[1, half, at, f, 2:4, :] = mixed[depth - 2 :, :]
-    send_part(1)
+    send_message(1)
+    send_message(2)
 
     def fringe_left(i, _):
         fringe_copy(i, me_b, me_b).wait_send()
@@ -426,13 +432,13 @@
         downward.wait_send()
 
     loaded("linv", "right")
-    def arrive(half, g):
-        source = half * n_a + g
-        for part in range(2):
-            sized(third, lambda count: fwd_copy(part, half, g, source, count).wait_recv())
-        return 0
-
-    each_source(arrive)
+    def await_message(message):
+        _, first, count = MESSAGES[message]
+        each_source(
+            lambda half, g: sized(
+                first, count, third, lambda n: fwd_copy(message, half, g, half * n_a + g, n).wait_recv()
+            )
+        )
 
     def solve(f):
         for p in range(n_pen):
@@ -449,43 +455,60 @@
         for p in range(n_pen):
             solved_line[p, f] = line[p * depth : (p + 1) * depth, :]
 
-    solve(0)
-    solve(1)
-
-    @pl.when(third)
-    def _():
-        solve(2)
-
-    def back_copy(peer, half, g, count):
+    def back_copy(answer, peer, half, g, count):
+        first = ANSWERS[answer][0]
         return pltpu.make_async_remote_copy(
-            src_ref=solved_line.at[peer, pl.ds(0, count)],
-            dst_ref=solved.at[half, g, pl.ds(0, count)],
-            send_sem=back_send.at[peer],
-            recv_sem=back_recv.at[half * n_a + g],
+            src_ref=solved_line.at[peer, pl.ds(first, count)],
+            dst_ref=solved.at[half, g, pl.ds(first, count)],
+            send_sem=back_send.at[answer, peer],
+            recv_sem=back_recv.at[answer, half * n_a + g],
             device_id={"pen": peer},
             device_id_type=MESH,
         )
 
-    each_peer(
-        lambda half, g: sized(third, lambda count: back_copy(half * n_a + g, zh, a, count).start())
-    )
-
-    def keep_solved(count):
-        solved[zh, a, 0:count] = solved_line[me_p, 0:count]
-
-    sized(third, keep_solved)
+    def send_answer(answer):
+        first, count = ANSWERS[answer]
+        each_peer(
+            lambda half, g: sized(
+                first, count, third, lambda n: back_copy(answer, half * n_a + g, zh, a, n).start()
+            )
+        )
+
+        def keep_solved(n):
+            solved[zh, a, first : first + n] = solved_line[me_p, first : first + n]
+
+        sized(first, count, third, keep_solved)
+
+    await_message(0)
+    await_message(1)
+    solve(0)
+    send_answer(0)
+    await_message(2)
+    solve(1)
+
+    @pl.when(third)
+    def _():
+        solve(2)
+
+    send_answer(1)
 
     def left(half, g):
-        for part in range(2):
-            sized(takes_third(half, g), lambda count: fwd_copy(part, half, g, me_p, count).wait_send())
-        return sized(third, lambda count: back_copy(half * n_a + g, zh, a, count).wait_send())
+        for message, (_, first, count) in enumerate(MESSAGES):
+            sized(first, count, takes_third(half, g), lambda n: fwd_copy(message, half, g, me_p, n).wait_send())
+        for answer, (first, count) in enumerate(ANSWERS):
+            sized(first, count, third, lambda n: back_copy(answer, half * n_a + g, zh, a, n).wait_send())
+        return 0
 
     each_peer(left)
-    each_source(
-        lambda half, g: sized(
-            takes_third(half, g), lambda count: back_copy(half * n_a + g, half, g, count).wait_recv()
-        )
-    )
+
+    def answered(half, g):
+        for answer, (first, count) in enumerate(ANSWERS):
+            sized(
+                first, count, takes_third(half, g), lambda n: back_copy(answer, half * n_a + g, half, g, n).wait_recv()
+            )
+        return 0
+
+    each_source(answered)
 
     def solved_at(n, g):
         return solved[place_of(n, g)]
@@ -544,7 +567,7 @@
                 pltpu.SMEM((1, LANES), jnp.int32),
                 dma(()),
                 pltpu.VMEM((WIDE, LANES), jnp.bfloat16),
-                pltpu.VMEM((n_blk, WIDE, LANES), jnp.bfloat16),
+                pltpu.VMEM((n_blk, LANES, WIDE), jnp.bfloat16),
                 pltpu.VMEM((2 * nf * n_hi, WIDE), jnp.bfloat16),
                 pltpu.VMEM(((2 * nf + 1) * n_hi, WIDE), f32),
                 pltpu.VMEM((n_blk, nf, cap), f32),
@@ -562,10 +585,10 @@
                 dma((n_blk,)),
                 dma((2,)),
                 dma((2,)),
+                dma((3, n_pen)),
+                dma((3, n_pen)),
                 dma((2, n_pen)),
                 dma((2, n_pen)),
-                dma((n_pen,)),
-                dma((n_pen,)),
             ],
             compiler_params=pltpu.CompilerParams(
                 collective_id=0, has_side_effects=True, vmem_limit_bytes=60 * 1024 * 1024

time: 63 us -> 63.3 us (level)
  no operation moved by 1% of the time
where the time goes in v4:
time: 63.3 us; the launch traced here: 63.1 us
  Pallas kernels  61.5 us (97%)
  local copies, waits for them, and re-layouts  1.59 us (3%)
    pallas_call x1, Pallas kernels, shards(): pl.pallas_call(functools.partial(kernel, n_blk, n_pen), out_shape=jax.Sha...  61.5 us
    unnamed x1, local copies, waits for them, and re-layouts  1.59 us

profile of v4, /device:TPU:1, one launch (start us, length us, event | category | flops | bytes accessed | tf_op | source)
XLA Modules:
  0.0 63.1 jit_solution(18189113492069872742)
XLA Ops:
  0.0 61.5 %shard_map.118 = f32[5,8,1024]{2,1,0:T(8,128)} custom-call(s32[32]{0:T(128)} %owner_hbm.1, s32[32]{0:T(128)} %bitcast.33, f32[5,8,1024]{2,1,0:T(8,128)} %bitcast.24, f32[5,8,1024]{2,1,0:T(8,128)} %bitcast.25, s32[8,1024]{1,0:T(8,128)} %bitcast.30, s32[32,8,128]{2,1,0:T(8,128)} %bitcast.26, f32[32,8,128]{2,1,0:T(8,128)} %bitcast.27, s32[32,128]{1,0:T(8,128)} %bitcast.32, ...), custom_call_target="tpu_custom_call" | custom-call | tf_op jit(solution)/shard_map/pallas_call | solution.py:547
  61.5 1.6 %copy.14 = f32[1,8,5,1024]{3,1,2,0:T(8,128)} copy(f32[1,8,5,1024]{3,1,2,0:T(8,128)} %bitcast.22) | data formatting | bytes 327680

commit v5 on v4

--- a/solution.py
+++ b/solution.py
@@ -11,7 +11,7 @@
 LANES = 128
 DEAD = 1e30
 WIDE = 256
-TOGETHER = 4
+TOGETHER = 8
 PLACED = 4
 
 
@@ -191,11 +191,23 @@
         slots = jnp.concatenate([slots] * (WIDE // LANES), axis=1)
         recv_lanes[b] = jnp.where(slots == across, 1.0, 0.0).astype(jnp.bfloat16)
 
-    def interpolate(q, send, count):
-        for u in range(TOGETHER):
-            receivers(q * TOGETHER + u)
-        for u in range(count):
-            slot = q * TOGETHER + u
+    def send_ready(slot, _):
+        fringe_copy(slot, lax.rem(me_b + fringe_offset(slot), n_blk), me_b).start()
+        return 0
+
+    together = min(TOGETHER, n_blk)
+    steps = n_blk // together
+
+    def interpolate(q, _):
+        @pl.when(q == steps // 2)
+        def _():
+            met()
+            lax.fori_loop(0, steps // 2 * together, send_ready, 0)
+
+        for u in range(together):
+            receivers(q * together + u)
+        for u in range(together):
+            slot = q * together + u
             peer = lax.rem(me_b + fringe_offset(slot), n_blk)
             block = held_ref[0, peer]
             cells, weights = dcell_ref[block], dweight_ref[block]
@@ -218,23 +230,19 @@
                     row = jnp.where(live, row, DEAD)
                 rows_out[slot, pl.ds(m, 1), :] = row
 
-        if send:
-            for u in range(count):
-                send_ready(q * TOGETHER + u, 0)
-        return 0
-
-    def send_ready(slot, _):
-        fringe_copy(slot, lax.rem(me_b + fringe_offset(slot), n_blk), me_b).start()
-        return 0
-
-    steps = n_blk // TOGETHER
+        @pl.when(q >= steps // 2)
+        def _():
+            for u in range(together - 1):
+                send_ready(q * together + u, 0)
+
+            @pl.when(q < steps - 1)
+            def _():
+                send_ready(q * together + together - 1, 0)
+
+        return 0
+
     loaded("rcell")
-    lax.fori_loop(0, steps // 2, lambda q, _: interpolate(q, False, TOGETHER), 0)
-    met()
-    lax.fori_loop(0, steps // 2 * TOGETHER, send_ready, 0)
-    lax.fori_loop(steps // 2, steps - 1, lambda q, _: interpolate(q, True, TOGETHER), 0)
-    interpolate(steps - 1, True, TOGETHER - 1)
-
+    lax.fori_loop(0, steps, interpolate, 0)
     rows_in[me_b] = jnp.full(rows_in.shape[1:], DEAD, f32)
 
     placed[...] = jnp.zeros_like(placed)
@@ -338,8 +346,8 @@
     def takes_third(half, g):
         return lax.rem(g, 2) == half
 
-    MESSAGES = ((0, 0, 2), (1, 0, 1), (1, 1, 1))
-    ANSWERS = ((0, 1), (1, 1))
+    MESSAGES = ((0, 0, 2), (1, 0, 2))
+    ANSWERS = ((0, 2),)
 
     def sized(first, count, more, do):
         if first + count < 2:
@@ -415,7 +423,6 @@
             work[1, half, at, f, 0:2, :] = mixed[0:2, :]
             work[1, half, at, f, 2:4, :] = mixed[depth - 2 :, :]
     send_message(1)
-    send_message(2)
 
     def fringe_left(i, _):
         fringe_copy(i, me_b, me_b).wait_send()
@@ -482,15 +489,13 @@
     await_message(0)
     await_message(1)
     solve(0)
+    solve(1)
+
+    @pl.when(third)
+    def _():
+        solve(2)
+
     send_answer(0)
-    await_message(2)
-    solve(1)
-
-    @pl.when(third)
-    def _():
-        solve(2)
-
-    send_answer(1)
 
     def left(half, g):
         for message, (_, first, count) in enumerate(MESSAGES):
@@ -585,10 +590,10 @@
                 dma((n_blk,)),
                 dma((2,)),
                 dma((2,)),
-                dma((3, n_pen)),
-                dma((3, n_pen)),
                 dma((2, n_pen)),
                 dma((2, n_pen)),
+                dma((1, n_pen)),
+                dma((1, n_pen)),
             ],
             compiler_params=pltpu.CompilerParams(
                 collective_id=0, has_side_effects=True, vmem_limit_bytes=60 * 1024 * 1024

time: 63.3 us -> 62.4 us (0.986)
  Pallas kernels: 61.5 us -> 60.8 us
    pallas_call x1, Pallas kernels: 61.5 us -> 60.8 us  [shards(): pl.pallas_call(functools.partial(kernel, n_blk, n_pen), out_shape=jax.Sha...]
where the time goes in v5:
time: 62.4 us
  Pallas kernels  60.8 us (97%)
  local copies, waits for them, and re-layouts  1.59 us (3%)
    pallas_call x1, Pallas kernels, shards(): pl.pallas_call(functools.partial(kernel, n_blk, n_pen), out_shape=jax.Sha...  60.8 us
    unnamed x1, local copies, waits for them, and re-layouts  1.59 us

profile of v5, /device:TPU:1, one launch (start us, length us, event | category | flops | bytes accessed | tf_op | source)
XLA Modules:
  0.0 62.4 jit_solution(2950899769507485601)
XLA Ops:
  0.0 60.8 %shard_map.118 = f32[5,8,1024]{2,1,0:T(8,128)} custom-call(s32[32]{0:T(128)} %owner_hbm.1, s32[32]{0:T(128)} %bitcast.33, f32[5,8,1024]{2,1,0:T(8,128)} %bitcast.24, f32[5,8,1024]{2,1,0:T(8,128)} %bitcast.25, s32[8,1024]{1,0:T(8,128)} %bitcast.30, s32[32,8,128]{2,1,0:T(8,128)} %bitcast.26, f32[32,8,128]{2,1,0:T(8,128)} %bitcast.27, s32[32,128]{1,0:T(8,128)} %bitcast.32, ...), custom_call_target="tpu_custom_call" | custom-call | tf_op jit(solution)/shard_map/pallas_call | solution.py:552
  60.8 1.6 %copy.14 = f32[1,8,5,1024]{3,1,2,0:T(8,128)} copy(f32[1,8,5,1024]{3,1,2,0:T(8,128)} %bitcast.22) | data formatting | bytes 327680

commit v6 on v5

--- a/solution.py
+++ b/solution.py
@@ -12,7 +12,7 @@
 DEAD = 1e30
 WIDE = 256
 TOGETHER = 8
-PLACED = 4
+PLACED = 8
 
 
 def split(value):
@@ -247,11 +247,13 @@
 
     placed[...] = jnp.zeros_like(placed)
 
+    group = min(PLACED, n_blk)
+
     def place(q, _):
-        sources = [lax.rem(me_b - fringe_offset(q * PLACED + u) + n_blk, n_blk) for u in range(PLACED)]
-        for u in range(PLACED - 1):
-            fringe_copy(q * PLACED + u, sources[u], sources[u]).wait_recv()
-        last = q * PLACED + PLACED - 1
+        sources = [lax.rem(me_b - fringe_offset(q * group + u) + n_blk, n_blk) for u in range(group)]
+        for u in range(group - 1):
+            fringe_copy(q * group + u, sources[u], sources[u]).wait_recv()
+        last = q * group + group - 1
 
         @pl.when(last < n_blk - 1)
         def _():
@@ -271,7 +273,7 @@
         )
         return 0
 
-    lax.fori_loop(0, n_blk // PLACED, place, 0)
+    lax.fori_loop(0, n_blk // group, place, 0)
     for m in range(nf):
         for w in range(wides):
             at, lanes = m * n_hi + w * depth, slice(w * WIDE, (w + 1) * WIDE)

time: 62.4 us -> 62.6 us (level)
  no operation moved by 1% of the time
where the time goes in v6:
time: 62.6 us; the launch traced here: 62.5 us
  Pallas kernels  60.9 us (97%)
  local copies, waits for them, and re-layouts  1.59 us (3%)
    pallas_call x1, Pallas kernels, shards(): pl.pallas_call(functools.partial(kernel, n_blk, n_pen), out_shape=jax.Sha...  60.9 us
    unnamed x1, local copies, waits for them, and re-layouts  1.59 us

profile of v6, /device:TPU:1, one launch (start us, length us, event | category | flops | bytes accessed | tf_op | source)
XLA Modules:
  0.0 62.5 jit_solution(2981536760230179723)
XLA Ops:
  0.0 60.9 %shard_map.118 = f32[5,8,1024]{2,1,0:T(8,128)} custom-call(s32[32]{0:T(128)} %owner_hbm.1, s32[32]{0:T(128)} %bitcast.33, f32[5,8,1024]{2,1,0:T(8,128)} %bitcast.24, f32[5,8,1024]{2,1,0:T(8,128)} %bitcast.25, s32[8,1024]{1,0:T(8,128)} %bitcast.30, s32[32,8,128]{2,1,0:T(8,128)} %bitcast.26, f32[32,8,128]{2,1,0:T(8,128)} %bitcast.27, s32[32,128]{1,0:T(8,128)} %bitcast.32, ...), custom_call_target="tpu_custom_call" | custom-call | tf_op jit(solution)/shard_map/pallas_call | solution.py:554
  60.9 1.6 %copy.14 = f32[1,8,5,1024]{3,1,2,0:T(8,128)} copy(f32[1,8,5,1024]{3,1,2,0:T(8,128)} %bitcast.22) | data formatting | bytes 327680
